TPU v7x, 256 devices: a whole 4x4x8 slice. The times are simulated.
256 devices in a mesh: row: 64 (over z, y, core), col: 4 (over x).
Axes of the slice: x: 4, y: 4, z: 8, core: 2. Of those that a mesh axis runs over, the one named last changes fastest.
Arguments:
- right_sides: float32 [8, 3, 40960], P(None, None, ('row', 'col')), may hold values from -20 to 20
- cosine: float32 [40960], P(('row', 'col')), may hold values from -1 to 1
- azimuth: float32 [40960], P(('row', 'col')), may hold values from -3.140625 to 3.140625
- radius: float32 [40960], P(('row', 'col')), may hold values from 0.97 to 1.03
- panel_area: float32 [40960], P(('row', 'col')), may hold values from 0.5 to 2
Outputs:
- next_block: float32 [8, 3, 40960], P(None, None, ('row', 'col'))
- coefficients: float32 [24, 8], replicated
All inputs are finite; a program needn't handle non-finite values.
Results may differ from a plain program's by a relative error of at most 0.0003.
Values sent between devices are 32-bit elements; how exact they have to be, the bound alone decides.
A program may use at most 192 MiB of HBM per device.

v0:
```python
import functools
import math

import jax
import jax.numpy as jnp
from jax import lax
from jax.experimental import pallas as pl
from jax.experimental.pallas import tpu as pltpu
from jax.sharding import PartitionSpec as P

f32 = jnp.float32
bf16 = jnp.bfloat16
MESH = pl.DeviceIdType.MESH
NEAREST = (1, 7, 2, 6, 3, 5, 4)
LINE = 4
GROUP = 16
WIDTH = 160
SOURCES = GROUP * WIDTH
TARGETS = GROUP * WIDTH
COLS = 256
DEPTH = 512
CHUNK = 32
FEATS = 80
TARGET_TILES = TARGETS // COLS
SOURCE_TILES = SOURCES // DEPTH


def exact_dot(left, right, dims):
    return lax.dot_general(
        left, right, (dims, ((), ())), precision=lax.Precision.HIGHEST, preferred_element_type=f32
    )


def split(value, pieces):
    parts = []
    for _ in range(pieces):
        part = value.astype(bf16).astype(f32)
        parts.append(part)
        value = value - part
    return parts


def eliminate(matrix):
    row = lax.broadcasted_iota(jnp.int32, matrix.shape, 0)
    for k in range(8):
        scale = 1.0 / jnp.sqrt(matrix[k : k + 1, k : k + 1])
        pivot = matrix[k : k + 1, :] * scale
        column = matrix[:, k : k + 1] * scale
        matrix = jnp.where(row == k, pivot, jnp.where(row > k, matrix - column * pivot, matrix))
    return matrix


def kernel(
    spacing,
    right_ref,
    cosine_ref,
    azimuth_ref,
    radius_ref,
    area_ref,
    next_ref,
    coef_ref,
    src_buf,
    tgt_buf,
    columns,
    feats,
    rows,
    tile_a,
    tile_b,
    sums,
    outbox,
    inbox,
    gb_buf,
    ga_buf,
    sz_send,
    sz_recv,
    sc_send,
    sc_recv,
    tgt_send,
    tgt_recv,
    out_send,
    out_recv,
    gb_send,
    gb_recv,
    ga_send,
    ga_recv,
):
    me_row = lax.axis_index("row")
    me_x = lax.axis_index("col")
    core = lax.rem(me_row, 2)
    me_y = lax.rem(lax.div(me_row, 2), LINE)
    me_z = lax.div(me_row, 8)
    me_a = core * 8 + me_z
    me_b = me_y * LINE + me_x

    def peer_z(slot):
        return (slot * 8 + me_y * 2 + core, me_x)

    def peer_core(slot):
        return (me_z * 8 + me_y * 2 + slot, me_x)

    def peer_a(slot):
        return (lax.rem(slot, 8) * 8 + me_y * 2 + lax.div(slot, 8), me_x)

    def peer_b(slot):
        return (me_z * 8 + lax.div(slot, LINE) * 2 + core, lax.rem(slot, LINE))

    lines = ((peer_z, me_z, 8), (peer_core, core, 2), (peer_b, me_b, GROUP), (peer_a, me_a, GROUP))
    barrier = pltpu.get_barrier_semaphore()
    for peer, mine, count in lines[:3]:

        def greet(k, carry, peer=peer, mine=mine, count=count):
            pl.semaphore_signal(
                barrier, inc=1, device_id=peer(lax.rem(mine + k, count)), device_id_type=MESH
            )
            return carry

        lax.fori_loop(1, count, greet, 0)

    class Exchange:
        def __init__(self, line, src_of, dst_of, send, recv):
            self.peer, self.mine, self.count = lines[line]
            self.src_of, self.dst_of, self.send, self.recv = src_of, dst_of, send, recv

        def copy(self, slot, landing):
            return pltpu.make_async_remote_copy(
                src_ref=self.src_of(slot),
                dst_ref=self.dst_of(landing),
                send_sem=self.send.at[slot],
                recv_sem=self.recv.at[landing],
                device_id=self.peer(slot),
                device_id_type=MESH,
            )

        def each(self, act):
            def one(k, carry):
                act(lax.rem(self.mine + k, self.count))
                return carry

            lax.fori_loop(1, self.count, one, 0)

        def start(self):
            far_first = sorted(range(1, self.count), key=lambda k: (-min(k, self.count - k), k))
            for k in far_first:
                self.copy(lax.rem(self.mine + k, self.count), self.mine).start()

        def wait(self):
            self.each(lambda slot: self.copy(slot, slot).wait_recv())

        def finish(self):
            self.each(lambda slot: self.copy(slot, slot).wait_send())

    def group(buf, slot, count):
        return buf.at[pl.ds(slot * count, count)]

    src_z = Exchange(
        0, lambda s: src_buf.at[me_a], lambda s: src_buf.at[core * 8 + s], sz_send, sz_recv
    )
    src_core = Exchange(
        1, lambda s: group(src_buf, core, 8), lambda s: group(src_buf, s, 8), sc_send, sc_recv
    )
    tgt = Exchange(2, lambda s: tgt_buf.at[me_b], lambda s: tgt_buf.at[s], tgt_send, tgt_recv)
    out = Exchange(2, lambda s: outbox.at[s], lambda s: inbox.at[s], out_send, out_recv)
    sum_b = Exchange(2, lambda s: gb_buf.at[me_b], lambda s: gb_buf.at[s], gb_send, gb_recv)
    sum_a = Exchange(3, lambda s: ga_buf.at[me_a], lambda s: ga_buf.at[s], ga_send, ga_recv)

    cosine = cosine_ref[...]
    azimuth = azimuth_ref[...]
    radius = radius_ref[...]
    area = area_ref[...]
    sine_part = jnp.sqrt(jnp.maximum(1.0 - cosine * cosine, 0.0))
    pos0 = radius * (sine_part * jnp.cos(azimuth))
    pos1 = radius * (sine_part * jnp.sin(azimuth))
    pos2 = radius * cosine
    weight = (-0.75 / math.pi) * (area * spacing) / (2.0 * radius)
    nothing = jnp.zeros((3, WIDTH), f32)
    geo = jnp.concatenate([pos0, pos1, pos2, radius * radius, weight, nothing], axis=0)
    parts = [right_ref[m] for m in range(3)] + [geo]
    own_rest = jnp.concatenate([part[:, 128:WIDTH] for part in parts], axis=1)
    for m in range(4):
        src_buf[me_a, 8 * m : 8 * m + 8, :] = parts[m][:, :128]
    src_buf[me_a, 32:40, :] = own_rest
    tgt_buf[me_b, 0:4, :] = geo[0:4, :128]
    tgt_buf[me_b, 4:5, :] = jnp.concatenate([geo[a : a + 1, 128:WIDTH] for a in range(4)], axis=1)

    pl.semaphore_wait(barrier, sum(count - 1 for _, _, count in lines[:3]))
    def same_y(act):
        for k in range(1, LINE):
            act(me_y * LINE + lax.rem(me_x + k, LINE))

    def other_y(act):
        def one(k, carry):
            y = lax.rem(me_y + 1 + lax.div(k, LINE), LINE)
            act(y * LINE + lax.rem(me_x + k, LINE))
            return carry

        lax.fori_loop(0, GROUP - LINE, one, 0)

    def tgt_start(slot):
        tgt.copy(slot, me_b).start()

    def tgt_wait(slot):
        tgt.copy(slot, slot).wait_recv()

    same_y(tgt_start)
    for k in NEAREST[:3]:
        src_z.copy(lax.rem(me_z + 8 - k, 8), me_z).start()
    other_y(tgt_start)
    for k in NEAREST[3:]:
        src_z.copy(lax.rem(me_z + 8 - k, 8), me_z).start()

    def put_sources(tile, place, parts):
        lanes = slice(128 * place, 128 * place + 128)
        geo = parts[3]
        scaled = [split(parts[c] * geo[4:5, :], 2) for c in range(3)]
        along = sum(geo[c : c + 1, :] * (scaled[c][0] + scaled[c][1]) for c in range(3))
        pieces = [scaled[c][p] for p in range(2) for c in range(3)] + split(along, 3)
        pieces.append(jnp.zeros((8, 128), f32))
        feats[tile, :, lanes] = jnp.concatenate(pieces, axis=0).astype(bf16)
        at = pl.ds(pl.multiple_of(tile * DEPTH + 128 * place, 128), 128)
        for a in range(4):
            columns[a, at, :] = jnp.transpose(jnp.broadcast_to(geo[a : a + 1, :], (128, 128)))

    def put_tile(tile, quads):
        for place, parts in enumerate(quads):
            put_sources(tile, place, parts)
    def main_sources(tile, slots):
        put_tile(tile, [[src_buf[slot, 8 * m : 8 * m + 8, :] for m in range(4)] for slot in slots])

    def rest_sources():
        quads = [
            [
                jnp.concatenate(
                    [src_buf[4 * place + d, 32:40, 32 * m : 32 * m + 32] for d in range(4)], axis=1
                )
                for m in range(4)
            ]
            for place in range(4)
        ]
        put_tile(4, quads)

    for tile in range(TARGET_TILES):
        sums[tile] = jnp.zeros((3, FEATS, COLS), f32)

    def line_sources(tile, offsets):
        for k in offsets:
            slot = lax.rem(me_z + k, 8)
            src_z.copy(slot, slot).wait_recv()
        own = [me_z] if tile == 0 else []
        main_sources(
            tile, [core * 8 + slot for slot in own + [lax.rem(me_z + k, 8) for k in offsets]]
        )

    line_sources(0, NEAREST[:3])
    def main_rows(tile):
        rows[tile] = jnp.concatenate([tgt_buf[2 * tile], tgt_buf[2 * tile + 1]], axis=1)

    def all_rows():
        for tile in range(8):
            main_rows(tile)
        for tile in range(2):
            for a in range(4):
                rows[8 + tile, a : a + 1, :] = jnp.concatenate(
                    [tgt_buf[8 * tile + d, 4:5, 32 * a : 32 * a + 32] for d in range(8)], axis=1
                )

    same_y(tgt_wait)
    for tile in range(2):
        main_rows(2 * me_y + tile)

    def pair_parts(target_tile, source_tile, tile_ref):
        target = [rows[target_tile, a : a + 1, :] for a in range(3)]
        reach = rows[target_tile, 3:4, :] + spacing

        def one(c):
            at = pl.ds(pl.multiple_of(source_tile * DEPTH + c * CHUNK, CHUNK), CHUNK)

            def column(a):
                value = columns[a, at, :]
                return jnp.concatenate([value] * (COLS // 128), axis=1)

            r = [target[a] - column(a) for a in range(3)]
            dist = (r[0] * r[0] + spacing) + r[1] * r[1] + r[2] * r[2]
            inv = lax.rsqrt(dist)
            inv2 = inv * inv
            strength = (((reach - column(3)) - dist) * inv) * (inv2 * inv2)
            for a in range(3):
                value = strength * r[a]
                high = value.astype(bf16)
                tile_ref[a, 0, c * CHUNK : (c + 1) * CHUNK, :] = high
                tile_ref[a, 1, c * CHUNK : (c + 1) * CHUNK, :] = (value - high.astype(f32)).astype(bf16)

        return [functools.partial(one, c) for c in range(DEPTH // CHUNK)]

    def sum_parts(target_tile, source_tile, tile_ref):
        def one(a):
            left = feats[source_tile]
            sums[target_tile, a] += jnp.dot(
                left, tile_ref[a, 0], preferred_element_type=f32
            ) + jnp.dot(left, tile_ref[a, 1], preferred_element_type=f32)

        return [functools.partial(one, a) for a in range(3)]

    def mixed(firsts, seconds):
        order = [((i + 0.5) / len(firsts), 0, f) for i, f in enumerate(firsts)]
        order += [((i + 0.3) / len(seconds), 1, f) for i, f in enumerate(seconds)]
        for _, _, f in sorted(order, key=lambda item: item[:2]):
            f()

    def images(tile):
        found = []
        for a in range(3):
            total = sums[tile, a]
            image = -(total[48:56] + total[56:64] + total[64:72])
            for c in range(3):
                image = image + rows[tile, c : c + 1, :] * (
                    total[8 * c : 8 * c + 8] + total[24 + 8 * c : 32 + 8 * c]
                )
            found.append(image)
        return found

    pairs = TARGET_TILES // 2
    turns = pairs * SOURCE_TILES

    def place_of(turn):
        source = lax.div(turn, pairs)
        pair = lax.rem(turn, pairs)
        near_first = jnp.where(pair == pairs - 1, pairs - 1, lax.rem(me_y + pair, LINE))
        near_last = jnp.where(pair == 0, pairs - 1, lax.rem(me_y + pair, LINE))
        return source, 2 * jnp.where(source == SOURCE_TILES - 1, near_last, near_first)

    first_source, first_target = place_of(0)
    for f in pair_parts(first_target, first_source, tile_a):
        f()

    def advance(turn, carry):
        source, target = place_of(turn)
        later_source, later_target = place_of(jnp.minimum(turn + 1, turns - 1))

        @pl.when(lax.rem(turn, pairs) == pairs - 1)
        def _():
            @pl.when(turn == pairs - 1)
            def _():
                line_sources(1, NEAREST[3:])
                src_core.start()

            @pl.when(turn == 2 * pairs - 1)
            def _():
                src_core.wait()

                def far(tile, carry):
                    main_sources(tile, [(1 - core) * 8 + (tile - 2) * 4 + k for k in range(4)])
                    return carry

                lax.fori_loop(2, 4, far, 0)
                rest_sources()

        @pl.when(turn < turns)
        def _():
            mixed(pair_parts(target + 1, source, tile_b), sum_parts(target, source, tile_a))

        @pl.when(turn == 0)
        def _():
            other_y(tgt_wait)
            all_rows()

        @pl.when(turn < turns + 1)
        def _():
            mixed(
                pair_parts(later_target, later_source, tile_a),
                sum_parts(target + 1, source, tile_b),
            )

        last = source == SOURCE_TILES - 1

        @pl.when(last)
        def _():
            @pl.when(target == 8)
            def _():
                for tile in range(2):
                    found = images(8 + tile)
                    for d in range(8):
                        lanes = slice(32 * d, 32 * d + 32)
                        outbox[8 * tile + d, 24:32, :] = jnp.concatenate(
                            [found[a][:, lanes] for a in range(3)] + [jnp.zeros((8, 32), f32)], axis=1
                        )

            @pl.when(target < 8)
            def _():
                for tile in range(2):
                    found = images(target + tile)
                    for half in range(2):
                        for a in range(3):
                            outbox[2 * (target + tile) + half, 8 * a : 8 * a + 8, :] = found[a][
                                :, 128 * half : 128 * half + 128
                            ]

            @pl.when(target < 8)
            def _():
                def push(x, carry):
                    slot = 2 * target + lax.rem(me_x + x, LINE)

                    @pl.when(slot != me_b)
                    def _():
                        out.copy(slot, me_b).start()

                    return carry

                lax.fori_loop(0, LINE, push, 0)

        return carry

    lax.fori_loop(0, turns, advance, 0)

    inbox[me_b] = outbox[me_b]
    for exchange in (tgt, src_z, src_core, out):
        exchange.finish()
    out.wait()
    image = inbox[0]
    for slot in range(1, GROUP):
        image = image + inbox[slot]

    lane = lax.broadcasted_iota(jnp.int32, (8, 128), 1)
    own = [src_buf[me_a, 8 * m : 8 * m + 8, :] for m in range(3)]
    own.append(jnp.where(lane < 96, src_buf[me_a, 32:40, :], 0.0))
    right = jnp.concatenate(own, axis=1)
    pushed = jnp.concatenate([image[8 * m : 8 * m + 8, :] for m in range(4)], axis=1)
    both = jnp.concatenate([right, pushed], axis=0)
    gram = exact_dot(both, both, ((1,), (1,)))
    gram = jnp.concatenate([gram[0:8], gram[8:16]], axis=1)
    gram = jnp.concatenate([gram[2 * m : 2 * m + 2] for m in range(4)], axis=1)
    for total, buf in ((sum_b, gb_buf), (sum_a, ga_buf)):
        buf[total.mine] = gram
        total.start()
        total.wait()
        gram = buf[0]
        for slot in range(1, GROUP):
            gram = gram + buf[slot]
    gram = jnp.concatenate([gram[:, 32 * m : 32 * m + 32] for m in range(4)], axis=0)

    row8 = lax.broadcasted_iota(jnp.int32, (8, 8), 0)
    lane8 = lax.broadcasted_iota(jnp.int32, (8, 8), 1)
    unit = jnp.where(row8 == lane8, 1.0, 0.0)
    first = eliminate(jnp.concatenate([gram[:, 0:8], unit, gram[:, 8:16]], axis=1))
    inverse = first[:, 8:16]
    moved = exact_dot(first[:, 16:24], inverse, ((1,), (1,)))
    image_gram = exact_dot(
        exact_dot(inverse, gram[:, 24:32], ((1,), (0,))), inverse, ((1,), (1,))
    )
    remainder_gram = image_gram - exact_dot(moved, moved, ((0,), (0,)))
    back = exact_dot(moved, inverse, ((0,), (0,)))
    second = eliminate(jnp.concatenate([remainder_gram, inverse, -back], axis=1))
    stacked = jnp.concatenate([pushed, right], axis=0)
    result = exact_dot(second[:, 8:24], stacked, ((1,), (0,)))
    for c in range(3):
        next_ref[c, :, 0:128] = result[:, 128 * c : 128 * c + 128]
        next_ref[c, :, 128:WIDTH] = result[:, 384 + 32 * c : 416 + 32 * c]
    coef_ref[0:8, :] = jnp.where(lane8 >= row8, first[:, 0:8], 0.0)
    coef_ref[8:16, :] = moved + 0.5 * unit
    coef_ref[16:24, :] = jnp.where(lane8 >= row8, second[:, 0:8], 0.0)

    for exchange in (sum_b, sum_a):
        exchange.finish()


def shards(right_sides, cosine, azimuth, radius, panel_area):
    width = cosine.shape[0]
    total = width * lax.axis_size("row") * lax.axis_size("col")
    spacing = 4.0 * math.pi / total
    next_block, coefficients = pl.pallas_call(
        functools.partial(kernel, spacing),
        out_shape=(
            jax.ShapeDtypeStruct((3, 8, width), f32),
            jax.ShapeDtypeStruct((24, 8), f32),
        ),
        in_specs=[pl.BlockSpec(memory_space=pltpu.VMEM)] * 5,
        out_specs=(pl.BlockSpec(memory_space=pltpu.VMEM), pl.BlockSpec(memory_space=pltpu.VMEM)),
        scratch_shapes=[
            pltpu.VMEM((GROUP, 40, 128), f32),
            pltpu.VMEM((GROUP, 8, 128), f32),
            pltpu.VMEM((4, SOURCES, 128), f32),
            pltpu.VMEM((SOURCE_TILES, FEATS, DEPTH), bf16),
            pltpu.VMEM((TARGET_TILES, 8, COLS), f32),
            pltpu.VMEM((3, 2, DEPTH, COLS), bf16),
            pltpu.VMEM((3, 2, DEPTH, COLS), bf16),
            pltpu.VMEM((TARGET_TILES, 3, FEATS, COLS), f32),
            pltpu.VMEM((GROUP, 32, 128), f32),
            pltpu.VMEM((GROUP, 32, 128), f32),
            pltpu.VMEM((GROUP, 2, 128), f32),
            pltpu.VMEM((GROUP, 2, 128), f32),
        ]
        + [pltpu.SemaphoreType.DMA((GROUP,))] * 12,
        compiler_params=pltpu.CompilerParams(
            collective_id=0, has_side_effects=True, vmem_limit_bytes=40 << 20
        ),
        name="arnoldi_step",
    )(jnp.transpose(right_sides, (1, 0, 2)), *[v.reshape(1, width) for v in (cosine, azimuth, radius, panel_area)])
    return jnp.transpose(next_block, (1, 0, 2)), coefficients


def solution(mesh):
    placed = (
        P(None, None, ("row", "col")),
        P(("row", "col")),
        P(("row", "col")),
        P(("row", "col")),
        P(("row", "col")),
    )
    return jax.shard_map(
        shards,
        mesh=mesh,
        in_specs=placed,
        out_specs=(P(None, None, ("row", "col")), P()),
        check_vma=False,
    )
```

profile of v0, /device:TPU:1, one launch (start us, length us, event | category | flops | bytes accessed | tf_op | source)
XLA Modules:
  0.0 69.5 jit_solution(8430553250138834957)
XLA Ops:
  0.6 0.0 copy-start.4
  0.6 0.0 copy-start.2
  0.7 0.0 copy-start.3
  0.7 0.0 copy-start.1
  0.7 0.6 copy-done.4
  1.3 0.0 copy-done.2
  1.3 0.0 copy-done.3
  1.3 0.0 copy-done.1
  1.4 0.0 copy-start
  1.4 0.7 %copy-done = f32[8,3,160]{2,0,1:T(8,128)S(1)} copy-done((f32[8,3,160]{2,0,1:T(8,128)S(1)}, f32[8,3,160]{2,0,1:T(8,128)}, u32[]{:S(2)}) %copy-start) | copy-done | bytes 15384
  2.1 66.2 %arnoldi_step.1 = (f32[3,8,160]{2,1,0:T(8,128)S(1)}, f32[24,8]{1,0:T(8,128)S(1)}) custom-call(f32[3,8,160]{2,1,0:T(8,128)S(1)} %bitcast.6, f32[1,160]{1,0:T(1,128)S(1)} %bitcast.8, f32[1,160]{1,0:T(1,128)S(1)} %bitcast.9, f32[1,160]{1,0:T(1,128)S(1)} %bitcast.10, f32[1,160]{1,0:T(1,128)S(1)} %bitcast.11), custom_call_target="tpu_custom_call" | custom-call | tf_op jit(solution)/shard_map/arnoldi_step/pallas_call | solution.py:469
  68.3 0.7 copy.7
  68.9 0.6 copy.9
Async XLA Ops:
  0.6 0.7 copy-start.4
  0.6 0.7 copy-start.2
  0.7 0.7 copy-start.3
  0.7 0.7 %copy-start.1 = (f32[160]{0:T(256)S(1)}, f32[160]{0:T(256)}, u32[]{:S(2)}) copy-start(f32[160]{0:T(256)} %param.6) | copy-start | bytes 1924
  1.4 0.7 %copy-start = (f32[8,3,160]{2,0,1:T(8,128)S(1)}, f32[8,3,160]{2,0,1:T(8,128)}, u32[]{:S(2)}) copy-start(f32[8,3,160]{2,0,1:T(8,128)} %param.5) | copy-start | bytes 46084
where the time goes:
time: 69.7 us; the launch traced here: 69.5 us
  Pallas kernels  66.2 us (95%)
  local copies, waits for them, and re-layouts  2.7 us (4%)
    pallas_call x1, Pallas kernels, shards(): pl.pallas_call(functools.partial(kernel, spacing), out_shape=(jax.ShapeDt...  66.2 us
    unnamed x12, local copies, waits for them, and re-layouts  2.7 us

commit v1 on v0

--- a/solution.py
+++ b/solution.py
@@ -431,6 +431,7 @@
     for total, buf in ((sum_b, gb_buf), (sum_a, ga_buf)):
         buf[total.mine] = gram
         total.start()
+        total.finish()
         total.wait()
         gram = buf[0]
         for slot in range(1, GROUP):
@@ -457,9 +458,6 @@
     coef_ref[0:8, :] = jnp.where(lane8 >= row8, first[:, 0:8], 0.0)
     coef_ref[8:16, :] = moved + 0.5 * unit
     coef_ref[16:24, :] = jnp.where(lane8 >= row8, second[:, 0:8], 0.0)
-
-    for exchange in (sum_b, sum_a):
-        exchange.finish()
 
 
 def shards(right_sides, cosine, azimuth, radius, panel_area):

time: 69.7 us -> 69.4 us (level)
  no operation moved by 1% of the time
where the time goes in v1:
time: 69.4 us; the launch traced here: 69.3 us
  Pallas kernels  65.9 us (95%)
  local copies, waits for them, and re-layouts  2.7 us (4%)
    pallas_call x1, Pallas kernels, shards(): pl.pallas_call(functools.partial(kernel, spacing), out_shape=(jax.ShapeDt...  65.9 us
    unnamed x12, local copies, waits for them, and re-layouts  2.7 us

profile of v1, /device:TPU:1, one launch (start us, length us, event | category | flops | bytes accessed | tf_op | source)
XLA Modules:
  0.0 69.3 jit_solution(521808252968557361)
XLA Ops:
  0.6 0.0 copy-start.4
  0.6 0.0 copy-start.2
  0.7 0.0 copy-start.3
  0.7 0.0 copy-start.1
  0.7 0.6 copy-done.4
  1.3 0.0 copy-done.2
  1.3 0.0 copy-done.3
  1.3 0.0 copy-done.1
  1.4 0.0 copy-start
  1.4 0.7 %copy-done = f32[8,3,160]{2,0,1:T(8,128)S(1)} copy-done((f32[8,3,160]{2,0,1:T(8,128)S(1)}, f32[8,3,160]{2,0,1:T(8,128)}, u32[]{:S(2)}) %copy-start) | copy-done | bytes 15384
  2.1 65.9 %arnoldi_step.1 = (f32[3,8,160]{2,1,0:T(8,128)S(1)}, f32[24,8]{1,0:T(8,128)S(1)}) custom-call(f32[3,8,160]{2,1,0:T(8,128)S(1)} %bitcast.6, f32[1,160]{1,0:T(1,128)S(1)} %bitcast.8, f32[1,160]{1,0:T(1,128)S(1)} %bitcast.9, f32[1,160]{1,0:T(1,128)S(1)} %bitcast.10, f32[1,160]{1,0:T(1,128)S(1)} %bitcast.11), custom_call_target="tpu_custom_call" | custom-call | tf_op jit(solution)/shard_map/arnoldi_step/pallas_call | solution.py:467
  68.0 0.7 copy.7
  68.6 0.6 copy.9
Async XLA Ops:
  0.6 0.7 copy-start.4
  0.6 0.7 copy-start.2
  0.7 0.7 copy-start.3
  0.7 0.7 %copy-start.1 = (f32[160]{0:T(256)S(1)}, f32[160]{0:T(256)}, u32[]{:S(2)}) copy-start(f32[160]{0:T(256)} %param.6) | copy-start | bytes 1924
  1.4 0.7 %copy-start = (f32[8,3,160]{2,0,1:T(8,128)S(1)}, f32[8,3,160]{2,0,1:T(8,128)}, u32[]{:S(2)}) copy-start(f32[8,3,160]{2,0,1:T(8,128)} %param.5) | copy-start | bytes 46084
